TPU v7x, 32 devices: a whole 2x2x4 slice. The times are simulated.
32 devices in a mesh: dom: 8 (over z, y), tile: 4 (over x, core).
Axes of the slice: x: 2, y: 2, z: 4, core: 2. Of those that a mesh axis runs over, the one named last changes fastest.
Arguments:
- features: bfloat16 [16384, 256], P(('dom', 'tile')), may hold values from -6 to 6
- grad_out: bfloat16 [16384, 256], P(('dom', 'tile')), may hold values from -6 to 6
- self_weight: bfloat16 [256, 256], replicated, may hold values from -0.375 to 0.375
- neigh_weight: bfloat16 [256, 256], replicated, may hold values from -0.375 to 0.375
- edge_tiles: bfloat16 [2304, 128, 128], P(('dom', 'tile')), may hold values from 0 to 1.5, as said below
- tile_dst: int32 [2304], P(('dom', 'tile')), may hold values from 0 to 15
- tile_src: int32 [2304], P(('dom', 'tile')), may hold values from 0 to 25
- halo_send: int32 [8, 1024], P('dom'), may hold values from 0 to 2047
- hub_ids: int32 [256], P('dom'), may hold values from 0 to 2047
Outputs:
- activated: bfloat16 [16384, 256], P(('dom', 'tile'))
- grad_features: bfloat16 [16384, 256], P(('dom', 'tile'))
- grad_self_weight: float32 [256, 256], replicated
- grad_neigh_weight: float32 [256, 256], replicated
Inputs may be any that keep to these rules, and one draw needn't show every extreme that they name: `edge_tiles`: each entry is zero or an edge weight of 0.3 or more.
All inputs are finite; a program needn't handle non-finite values.
Results may differ from a plain program's by a relative error of at most 0.014.
Values may be sent and summed in bfloat16 or wider, within the bound.
A program may use at most 64 MiB of HBM per device.

v0:
```python
import jax
import jax.numpy as jnp
from jax import lax
from jax.sharding import PartitionSpec as P


def block_onehot(indices, number):
    return (indices[None, :] == jnp.arange(number, dtype=jnp.int32)[:, None]).astype(jnp.float32)


def on_device(
    features,
    grad_out,
    self_weight,
    neigh_weight,
    edge_tiles,
    tile_dst,
    tile_src,
    halo_send,
    hub_ids,
):
    domains = lax.axis_size("dom")
    groups = lax.axis_size("tile")
    quarter = features.shape[0]
    columns = features.shape[1]
    tile_size = edge_tiles.shape[1]
    halo_total = halo_send.shape[1]
    per_peer = halo_total // domains
    whole_rows = lax.all_gather(features, "tile", axis=0, tiled=True)
    vertices = whole_rows.shape[0]
    outgoing = whole_rows[halo_send[0]].reshape(domains, per_peer, columns)
    own_hubs = whole_rows[hub_ids]
    width = outgoing.shape[2]
    halo_rows = lax.all_to_all(outgoing, "dom", split_axis=0, concat_axis=0, tiled=True).reshape(
        halo_total, width
    )
    hub_rows = lax.all_gather(own_hubs, "dom", axis=0, tiled=True)
    boundary = jnp.concatenate([halo_rows, hub_rows], axis=0)
    source = jnp.concatenate([whole_rows, boundary], axis=0)
    src_rows = source.shape[0]
    src_blocks = src_rows // tile_size
    dst_blocks = vertices // tile_size
    picked = source.reshape(src_blocks, tile_size, columns)[tile_src]
    products = jnp.einsum("tij,tjf->tif", edge_tiles, picked, preferred_element_type=jnp.float32)
    into_dest = block_onehot(tile_dst, dst_blocks)
    partial_sum = jnp.einsum(
        "dt,tif->dif", into_dest, products, precision=lax.Precision.HIGHEST
    ).reshape(vertices, columns)
    row_weight = jnp.sum(edge_tiles, axis=2, dtype=jnp.float32)
    partial_degree = jnp.dot(into_dest, row_weight, precision=lax.Precision.HIGHEST).reshape(
        vertices
    )
    summed, degree = (
        lax.psum_scatter(
            partial_sum.astype(jnp.bfloat16), "tile", scatter_dimension=0, tiled=True
        ).astype(jnp.float32),
        lax.psum_scatter(
            partial_degree.astype(jnp.bfloat16), "tile", scatter_dimension=0, tiled=True
        ).astype(jnp.float32),
    )
    divisor = jnp.maximum(degree, 1.0)
    mean_rows = (summed / divisor[:, None]).astype(jnp.bfloat16)
    hidden = jnp.dot(features, self_weight, preferred_element_type=jnp.float32) + jnp.dot(
        mean_rows, neigh_weight, preferred_element_type=jnp.float32
    )
    activated = jax.nn.silu(hidden).astype(jnp.bfloat16)
    sigmoid_h = jax.nn.sigmoid(hidden)
    grad_hidden = (
        grad_out.astype(jnp.float32) * sigmoid_h * (1.0 + hidden * (1.0 - sigmoid_h))
    ).astype(jnp.bfloat16)
    self_term = jnp.einsum("nf,nh->fh", features, grad_hidden, preferred_element_type=jnp.float32)
    neigh_term = jnp.einsum("nf,nh->fh", mean_rows, grad_hidden, preferred_element_type=jnp.float32)
    grad_self_sum, grad_neigh_sum = lax.psum((self_term, neigh_term), ("dom", "tile"))
    inv_root = 1.0 / (quarter * groups * domains) ** 0.5
    grad_mean = lax.dot_general(
        grad_hidden, neigh_weight, (((1,), (1,)), ((), ())), preferred_element_type=jnp.float32
    )
    grad_mean_b = (grad_mean / divisor[:, None]).astype(jnp.bfloat16)
    grad_whole = lax.all_gather(grad_mean_b, "tile", axis=0, tiled=True)
    dst_pick = grad_whole.reshape(dst_blocks, tile_size, columns)[tile_dst]
    back_prod = jnp.einsum("tij,tif->tjf", edge_tiles, dst_pick, preferred_element_type=jnp.float32)
    into_source = block_onehot(tile_src, src_blocks)
    partial_src = jnp.einsum(
        "st,tjf->sjf", into_source, back_prod, precision=lax.Precision.HIGHEST
    ).reshape(src_rows, columns)
    grad_local = lax.psum_scatter(
        partial_src[:vertices].astype(jnp.bfloat16), "tile", scatter_dimension=0, tiled=True
    ).astype(jnp.float32)
    remote = lax.psum(partial_src[vertices:].astype(jnp.bfloat16), "tile").astype(jnp.float32)
    halo_grad = remote[:halo_total].reshape(domains, per_peer, width)
    hub_grad = remote[halo_total:]
    halo_back = (
        lax.all_to_all(
            halo_grad.astype(jnp.bfloat16), "dom", split_axis=0, concat_axis=0, tiled=True
        )
        .astype(halo_grad.dtype)
        .reshape(halo_total, width)
    )
    hub_back = lax.psum_scatter(hub_grad, "dom", scatter_dimension=0, tiled=True)
    spread = jnp.zeros((vertices, width), jnp.float32).at[halo_send[0]].add(halo_back)
    spread = spread.at[hub_ids].add(hub_back)
    own_spread = lax.dynamic_slice_in_dim(spread, lax.axis_index("tile") * quarter, quarter, 0)
    grad_features = (
        lax.dot_general(
            grad_hidden, self_weight, (((1,), (1,)), ((), ())), preferred_element_type=jnp.float32
        )
        + grad_local
        + own_spread
    )
    return (
        activated,
        grad_features.astype(jnp.bfloat16),
        grad_self_sum * inv_root,
        grad_neigh_sum * inv_root,
    )


def solution(mesh):
    return jax.shard_map(
        on_device,
        mesh=mesh,
        in_specs=(
            P(("dom", "tile"), None),
            P(("dom", "tile"), None),
            P(),
            P(),
            P(("dom", "tile"), None, None),
            P(("dom", "tile")),
            P(("dom", "tile")),
            P("dom", None),
            P("dom"),
        ),
        out_specs=(P(("dom", "tile"), None), P(("dom", "tile"), None), P(), P()),
        check_vma=False,
    )
```

profile of v0, /device:TPU:0, one launch (start us, length us, event | category | flops | bytes accessed | tf_op | source)
XLA Modules:
  0.0 453.9 jit_solution(10285785023682862956)
XLA Ops:
  8.6 20.4 %all-gather.4.cloned.1.call-done = bf16[2048,256]{1,0:T(8,128)(2,1)} async-done(((bf16[512,256]{1,0:T(8,128)(2,1)}), bf16[2048,256]{1,0:T(8,128)(2,1)}) %all-gather.4.cloned.1.call-update) | async-done | bytes 1048592 | tf_op jit(solution)/shard_map/all_gather | solution.py:29
  29.1 6.0 %gather_fusion = bf16[1024,256]{1,0:T(8,128)(2,1)} fusion(bf16[2048,256]{1,0:T(8,128)(2,1)} %all-gather.4.cloned.1.call-done, s32[1024]{0:T(1024)S(1)} %broadcast_clamp_fusion), kind=kCustom, calls=%fused_computation | custom fusion | bytes 1052672 | tf_op jit(solution)/shard_map/gather | solution.py:31
  35.1 5.5 %all-to-all-start = ((bf16[8,128,256]{2,1,0:T(8,128)(2,1)}), bf16[8,128,256]{2,1,0:T(8,128)(2,1)S(1)}, u32[]{:S(2)}, u32[]{:S(2)}) async-start(bf16[8,128,256]{2,1,0:T(8,128)(2,1)} %bitcast.3), calls=%async_computation | async-start | bytes 1048576 | tf_op jit(solution)/shard_map/all_to_all | solution.py:34
  41.4 36.8 %all-gather = bf16[256,256]{1,0:T(8,128)(2,1)S(1)} all-gather(bf16[32,256]{1,0:T(8,128)(2,1)S(1)} %gather_fusion.1), channel_id=2, replica_groups=mesh['dom'=8,'tile'=4] {'dom'}, dimensions={0}, use_global_device_ids=true | all-gather | bytes 147456 | tf_op jit(solution)/shard_map/all_gather | solution.py:37
  78.3 5.6 %gather_fusion.2 = bf16[72,128,256]{2,1,0:T(8,128)(2,1)} fusion(bf16[26,128,256]{2,1,0:T(8,128)(2,1)S(1)} %bitcast.45, s32[1024]{0:T(1024)S(1)} %pad_clamp_fusion.1), kind=kCustom, calls=%fused_computation.2 | custom fusion | bytes 9437472 | tf_op jit(solution)/shard_map/gather | solution.py:43
  83.9 8.2 %convolution_bitcast_fusion.1 = f32[72,128,256]{1,2,0:T(8,128)} fusion(bf16[72,128,256]{2,1,0:T(8,128)(2,1)} %gather_fusion.2, bf16[72,128,128]{2,1,0:T(8,128)(2,1)} %param.13), kind=kOutput, calls=%fused_computation.8 | convolution fusion | flops 603979776 | bytes 16515072 | tf_op jit(solution)/shard_map/tij,tjf->tif/dot_general | solution.py:44
  92.1 9.6 %copy.33 = f32[72,128,256]{2,0,1:T(8,128)} copy(f32[72,128,256]{1,2,0:T(8,128)} %convolution_bitcast_fusion.1) | data formatting | bytes 18874368 | tf_op jit(solution)/shard_map/tij,tjf->tif/dot_general | solution.py:44
  101.7 6.9 %convolution_convert_fusion.1 = bf16[16,128,256]{2,0,1:T(8,128)(2,1)S(1)} fusion(f32[72,128,256]{2,0,1:T(8,128)} %copy.33, s32[72]{0:T(128)S(1)} %copy-done.8), kind=kOutput, calls=%fused_computation.11 | convolution fusion | flops 453510272 | bytes 10486048 | tf_op jit(solution)/shard_map/dt,tif->dif/dot_general | solution.py:46
  108.7 1.3 copy.34
  112.2 5.9 %all-reduce = bf16[2048]{0:T(1024)(128)(2,1)S(1)} all-reduce(bf16[2048]{0:T(1024)(128)(2,1)S(1)} %fusion.3), channel_id=4, replica_groups=mesh['dom'=8,'tile'=4] {'tile'}, use_global_device_ids=true, to_apply=%region_2.0.clone | all-reduce | flops 2048 | bytes 8192
  118.5 13.0 %reduce-scatter.4.cloned.1.call-done = bf16[512,256]{1,0:T(8,128)(2,1)} async-done(((bf16[2048,256]{1,0:T(8,128)(2,1)}), bf16[512,256]{1,0:T(8,128)(2,1)}) %reduce-scatter.4.cloned.1.call-update) | async-done | bytes 262160 | tf_op jit(solution)/shard_map/reduce_scatter | solution.py:54
  131.4 2.2 multiply_convert_fusion
  133.6 1.0 fusion.2
  134.9 16.6 %all-gather.6.cloned.1.call-done = bf16[2048,256]{1,0:T(8,128)(2,1)} async-done(((bf16[512,256]{1,0:T(8,128)(2,1)}), bf16[2048,256]{1,0:T(8,128)(2,1)}) %all-gather.6.cloned.1.call-update) | async-done | bytes 1048592 | tf_op jit(solution)/shard_map/all_gather | solution.py:79
  151.5 6.8 %gather_fusion.3 = bf16[72,128,256]{2,1,0:T(8,128)(2,1)} fusion(bf16[16,128,256]{2,1,0:T(8,128)(2,1)} %bitcast.46, s32[1024]{0:T(1024)S(1)} %pad_clamp_fusion), kind=kCustom, calls=%fused_computation.3 | custom fusion | bytes 9437472 | tf_op jit(solution)/shard_map/gather | solution.py:80
  158.3 7.4 %convolution_bitcast_fusion = f32[72,128,256]{1,2,0:T(8,128)} fusion(bf16[72,128,256]{2,1,0:T(8,128)(2,1)} %gather_fusion.3, bf16[72,128,128]{2,1,0:T(8,128)(2,1)S(1)} %copy-done.3), kind=kOutput, calls=%fused_computation.7 | convolution fusion | flops 603979776 | bytes 16515072 | tf_op jit(solution)/shard_map/tij,tif->tjf/dot_general | solution.py:81
  165.7 9.6 %copy.36 = f32[72,128,256]{2,0,1:T(8,128)} copy(f32[72,128,256]{1,2,0:T(8,128)} %convolution_bitcast_fusion) | data formatting | bytes 18874368 | tf_op jit(solution)/shard_map/tij,tif->tjf/dot_general | solution.py:81
  175.4 7.7 %convolution_convert_fusion = bf16[26,128,256]{2,0,1:T(8,128)(2,1)S(1)} fusion(f32[72,128,256]{2,0,1:T(8,128)} %copy.36, s32[72]{0:T(128)S(1)} %copy-done.10), kind=kOutput, calls=%fused_computation.9 | convolution fusion | flops 736954176 | bytes 11141408 | tf_op jit(solution)/shard_map/st,tjf->sjf/dot_general | solution.py:83
  183.2 1.0 copy.38
  184.3 1.0 convolution_bitcast_fusion.2
  185.3 1.1 fusion.14
  186.4 31.8 %all-reduce.5.cloned.1.call-done = bf16[1280,256]{1,0:T(8,128)(2,1)} async-done(((bf16[1280,256]{1,0:T(8,128)(2,1)}), bf16[1280,256]{1,0:T(8,128)(2,1)}) %all-reduce.5.cloned.1.call-update) | async-done | bytes 655376 | tf_op jit(solution)/shard_map/psum | solution.py:89
  218.2 1.6 slice_convert_fusion
  220.0 1.3 copy.37
  222.2 5.7 %all-to-all-start.1 = ((bf16[8,128,256]{2,1,0:T(8,128)(2,1)}), bf16[8,128,256]{2,1,0:T(8,128)(2,1)S(1)}, u32[]{:S(2)}, u32[]{:S(2)}) async-start(bf16[8,128,256]{2,1,0:T(8,128)(2,1)} %bitcast.14), calls=%async_computation.3 | async-start | bytes 1048576 | tf_op jit(solution)/shard_map/all_to_all | solution.py:93
  227.9 126.8 %all-reduce.7.cloned.1.call-done = (f32[256,256]{0,1:T(8,128)}, f32[256,256]{0,1:T(8,128)}) async-done(((f32[256,256]{0,1:T(8,128)}, f32[256,256]{0,1:T(8,128)}), (f32[256,256]{0,1:T(8,128)}, f32[256,256]{0,1:T(8,128)})) %all-reduce.7.cloned.1.call-update) | async-done | bytes 524304 | tf_op jit(solution)/shard_map/psum | solution.py:73
  354.7 1.1 broadcast_multiply_fusion
  357.5 6.6 %scatter_custom_fusion = f32[2048,256]{1,0:T(8,128)S(1)} fusion(s32[1024]{0:T(1024)S(1)} %bitcast.53, bf16[1024,256]{1,0:T(8,128)(2,1)S(1)} %bitcast.50, f32[]{:T(128)} %constant.12.clone.1), kind=kCustom, calls=%fused_computation.21 | custom fusion | flops 524288 | bytes 2621444 | tf_op jit(solution)/shard_map/scatter-add | solution.py:100
  364.1 54.6 %reduce-scatter.8.cloned.1.call-done = f32[32,256]{1,0:T(8,128)} async-done(((f32[256,256]{1,0:T(8,128)}), f32[32,256]{1,0:T(8,128)}) %reduce-scatter.8.cloned.1.call-update) | async-done | bytes 32784 | tf_op jit(solution)/shard_map/reduce_scatter | solution.py:99
  418.7 1.8 scatter_fusion
  420.5 24.7 %reduce-scatter.6.cloned.1.call-done = bf16[512,256]{1,0:T(8,128)(2,1)} async-done(((bf16[2048,256]{1,0:T(8,128)(2,1)}), bf16[512,256]{1,0:T(8,128)(2,1)}) %reduce-scatter.6.cloned.1.call-update) | async-done | bytes 262160 | tf_op jit(solution)/shard_map/reduce_scatter | solution.py:86
  445.2 1.9 fusion.1
  (64 shorter events, 7.2 us)
Async XLA Ops:
  7.2 124.3 %copy-start = (bf16[256,256]{1,0:T(8,128)(2,1)S(1)}, bf16[256,256]{1,0:T(8,128)(2,1)}, u32[]{:S(2)}) copy-start(bf16[256,256]{1,0:T(8,128)(2,1)} %param.12) | copy-start | bytes 393220
  7.2 33.5 %copy-start.12 = (s32[32]{0:T(128)S(1)}, s32[32]{0:T(128)}, u32[]{:S(2)}) copy-start(s32[32]{0:T(128)} %param.17) | copy-start | bytes 388
  7.2 33.5 %copy-start.9 = (s32[72]{0:T(128)S(1)}, s32[72]{0:T(128)}, u32[]{:S(2)}) copy-start(s32[72]{0:T(128)} %param.15) | copy-start | bytes 868
  7.2 21.8 %all-gather.4.cloned.1.call-start = ((), (), s32[]{:S(2)}) async-start(), calls=%async_computation.5 | async-start | bytes 1310720 | tf_op jit(solution)/shard_map/all_gather | solution.py:29
  29.1 11.7 %copy-start.2 = (bf16[2048,256]{1,0:T(8,128)(2,1)S(1)}, bf16[2048,256]{1,0:T(8,128)(2,1)}, u32[]{:S(2)}) copy-start(bf16[2048,256]{1,0:T(8,128)(2,1)} %all-gather.4.cloned.1.call-done) | copy-start | bytes 3145732
  35.1 43.1 %all-to-all-start = ((bf16[8,128,256]{2,1,0:T(8,128)(2,1)}), bf16[8,128,256]{2,1,0:T(8,128)(2,1)S(1)}, u32[]{:S(2)}, u32[]{:S(2)}) async-start(bf16[8,128,256]{2,1,0:T(8,128)(2,1)} %bitcast.3), calls=%async_computation | async-start | bytes 1048576 | tf_op jit(solution)/shard_map/all_to_all | solution.py:34
  40.6 90.8 %reduce-scatter.4.cloned.1.call-start = ((), (), s32[]{:S(2)}) async-start(), calls=%async_computation.6 | async-start | bytes 1310720 | tf_op jit(solution)/shard_map/reduce_scatter | solution.py:54
  92.1 9.6 %copy-start.8 = (s32[72]{0:T(128)S(1)}, s32[72]{0:T(128)}, u32[]{:S(2)}) copy-start(s32[72]{0:T(128)} %param.14) | copy-start | bytes 868
  101.7 8.4 %copy-start.13 = (u32[32]{0:T(128)S(1)}, u32[32]{0:T(128)}, u32[]{:S(2)}) copy-start(u32[32]{0:T(128)} %constant.8) | copy-start | bytes 388
  108.7 2.7 copy-start.3
  108.7 9.5 %copy-start.4 = (bf16[512,256]{1,0:T(8,128)(2,1)S(1)}, bf16[512,256]{1,0:T(8,128)(2,1)}, u32[]{:S(2)}) copy-start(bf16[512,256]{1,0:T(8,128)(2,1)} %param.9) | copy-start | bytes 786436
  108.7 9.5 %copy-start.6 = (bf16[256,256]{1,0:T(8,128)(2,1)S(1)}, bf16[256,256]{1,0:T(8,128)(2,1)}, u32[]{:S(2)}) copy-start(bf16[256,256]{1,0:T(8,128)(2,1)} %param.11) | copy-start | bytes 393220
  110.1 41.4 %all-gather.6.cloned.1.call-start = ((), (), s32[]{:S(2)}) async-start(), calls=%async_computation.7 | async-start | bytes 1310720 | tf_op jit(solution)/shard_map/all_gather | solution.py:79
  134.6 83.6 %all-reduce.5.cloned.1.call-start = ((), (), s32[]{:S(2)}) async-start(), calls=%async_computation.9 | async-start | bytes 1310720 | tf_op jit(solution)/shard_map/psum | solution.py:89
  165.7 9.6 %copy-start.10 = (s32[72]{0:T(128)S(1)}, s32[72]{0:T(128)}, u32[]{:S(2)}) copy-start(s32[72]{0:T(128)} %param.15) | copy-start | bytes 868
  183.0 2.2 copy-start.11
  184.2 170.5 %all-reduce.7.cloned.1.call-start = ((), (), s32[]{:S(2)}) async-start(), calls=%async_computation.11 | async-start | bytes 1048576 | tf_op jit(solution)/shard_map/psum | solution.py:73
  186.4 232.4 %reduce-scatter.8.cloned.1.call-start = ((), (), s32[]{:S(2)}) async-start(), calls=%async_computation.10 | async-start | bytes 294912 | tf_op jit(solution)/shard_map/reduce_scatter | solution.py:99
  219.8 225.3 %reduce-scatter.6.cloned.1.call-start = ((), (), s32[]{:S(2)}) async-start(), calls=%async_computation.8 | async-start | bytes 1310720 | tf_op jit(solution)/shard_map/reduce_scatter | solution.py:86
  220.0 1.4 copy-start.5
  222.2 223.0 %copy-start.7 = (bf16[256,256]{1,0:T(8,128)(2,1)S(1)}, bf16[256,256]{1,0:T(8,128)(2,1)}, u32[]{:S(2)}) copy-start(bf16[256,256]{1,0:T(8,128)(2,1)} %param.11) | copy-start | bytes 393220
  222.2 135.2 %all-to-all-start.1 = ((bf16[8,128,256]{2,1,0:T(8,128)(2,1)}), bf16[8,128,256]{2,1,0:T(8,128)(2,1)S(1)}, u32[]{:S(2)}, u32[]{:S(2)}) async-start(bf16[8,128,256]{2,1,0:T(8,128)(2,1)} %bitcast.14), calls=%async_computation.3 | async-start | bytes 1048576 | tf_op jit(solution)/shard_map/all_to_all | solution.py:93
  227.9 219.2 %copy-start.1 = (bf16[256,256]{1,0:T(8,128)(2,1)S(1)}, bf16[256,256]{1,0:T(8,128)(2,1)}, u32[]{:S(2)}) copy-start(bf16[256,256]{1,0:T(8,128)(2,1)} %param.12) | copy-start | bytes 393220
Sparse Core Ops, SparseCore 0:
  9.6 19.4 all-gather.3
  110.2 21.1 reduce-scatter.3
  134.7 16.7 all-gather.5
  184.4 33.7 all-reduce.4
  225.0 129.7 all-reduce.6
  358.5 60.1 reduce-scatter.7
  421.2 23.9 reduce-scatter.5
where the time goes:
time: 455 us; the launch traced here: 454 us
  waiting for transfers between devices  289 us (64%)
  local copies, waits for them, and re-layouts  45.4 us (10%)
  blocking collectives  42.8 us (9%)
  matrix products  37.7 us (8%)
  between operations  15 us (3%)
  other arithmetic  12.7 us (3%)
  starting transfers between devices  11.6 us (3%)
    psum x1, waiting for transfers between devices, on_device(): lax.psum((self_term, neigh_term), ('dom', 'tile'))  127 us
    reduce_scatter x1, waiting for transfers between devices, on_device(): lax.psum_scatter(hub_grad, 'dom', scatter_dimension=0, tiled=True)  54.6 us
    all_gather x1, blocking collectives, on_device(): hub_rows = lax.all_gather(own_hubs, 'dom', axis=0, tiled=True)  36.8 us
    psum x1, waiting for transfers between devices, on_device(): lax.psum(partial_src[vertices:].astype(jnp.bfloat16), 'tile')  31.8 us
    reduce_scatter x1, waiting for transfers between devices, on_device(): lax.psum_scatter(partial_src[:vertices].astype(jnp.bfloat16), 'tile', sca...  24.7 us
    all_gather x1, waiting for transfers between devices, on_device(): whole_rows = lax.all_gather(features, 'tile', axis=0, tiled=True)  20.4 us
    all_gather x1, waiting for transfers between devices, on_device(): grad_whole = lax.all_gather(grad_mean_b, 'tile', axis=0, tiled=True)  16.6 us
    reduce_scatter x1, waiting for transfers between devices, on_device(): lax.psum_scatter(partial_sum.astype(jnp.bfloat16), 'tile', scatter_dimens...  13 us
  transfers between devices with their start and end apart: 9, of which 7 were waited for; matrix products, arithmetic and copies ran while one was open for 4% of the time, Pallas kernels for 0%

commit v1 on v0

--- a/solution.py
+++ b/solution.py
@@ -1,7 +1,17 @@
+import functools
 import jax
 import jax.numpy as jnp
 from jax import lax
 from jax.sharding import PartitionSpec as P
+
+
+def side_bring(x0, axis_tag, mesh_dim):
+    for pp in (axis_tag, mesh_dim):
+        x0 = lax.psum(x0, pp)
+    return x0
+
+
+launch_record_in = functools.partial(side_bring, axis_tag="tile", mesh_dim="dom")
 
 
 def block_onehot(indices, number):
@@ -70,7 +80,7 @@
     ).astype(jnp.bfloat16)
     self_term = jnp.einsum("nf,nh->fh", features, grad_hidden, preferred_element_type=jnp.float32)
     neigh_term = jnp.einsum("nf,nh->fh", mean_rows, grad_hidden, preferred_element_type=jnp.float32)
-    grad_self_sum, grad_neigh_sum = lax.psum((self_term, neigh_term), ("dom", "tile"))
+    grad_self_sum, grad_neigh_sum = launch_record_in((self_term, neigh_term))
     inv_root = 1.0 / (quarter * groups * domains) ** 0.5
     grad_mean = lax.dot_general(
         grad_hidden, neigh_weight, (((1,), (1,)), ((), ())), preferred_element_type=jnp.float32

time: 455 us -> 406 us (0.89)
  waiting for transfers between devices: 289 us -> 238 us
    psum x1 -> x2, waiting for transfers between devices: 127 us -> 74.5 us  [side_bring(): x0 = lax.psum(x0, pp)]
  transfers between devices with their start and end apart: 9 -> 10, of which waited for: 7 -> 8; matrix products, arithmetic and copies ran while one was open for 4% -> 13% of each run, Pallas kernels for 0% -> 0%
where the time goes in v1:
time: 406 us; the launch traced here: 405 us
  waiting for transfers between devices  238 us (59%)
  local copies, waits for them, and re-layouts  45.6 us (11%)
  blocking collectives  42.8 us (11%)
  matrix products  38.8 us (10%)
  between operations  15 us (4%)
  other arithmetic  12.7 us (3%)
  starting transfers between devices  11.7 us (3%)
    psum x2, waiting for transfers between devices, side_bring(): x0 = lax.psum(x0, pp)  74.5 us
    reduce_scatter x1, waiting for transfers between devices, on_device(): lax.psum_scatter(hub_grad, 'dom', scatter_dimension=0, tiled=True)  55 us
    all_gather x1, blocking collectives, on_device(): hub_rows = lax.all_gather(own_hubs, 'dom', axis=0, tiled=True)  36.8 us
    psum x1, waiting for transfers between devices, on_device(): lax.psum(partial_src[vertices:].astype(jnp.bfloat16), 'tile')  36.2 us
    reduce_scatter x1, waiting for transfers between devices, on_device(): lax.psum_scatter(partial_src[:vertices].astype(jnp.bfloat16), 'tile', sca...  24.7 us
    all_gather x1, waiting for transfers between devices, on_device(): whole_rows = lax.all_gather(features, 'tile', axis=0, tiled=True)  20.4 us
    all_gather x1, waiting for transfers between devices, on_device(): grad_whole = lax.all_gather(grad_mean_b, 'tile', axis=0, tiled=True)  13.6 us
    reduce_scatter x1, waiting for transfers between devices, on_device(): lax.psum_scatter(partial_sum.astype(jnp.bfloat16), 'tile', scatter_dimens...  13 us
  transfers between devices with their start and end apart: 10, of which 8 were waited for; matrix products, arithmetic and copies ran while one was open for 13% of the time, Pallas kernels for 0%

profile of v1, /device:TPU:0, one launch (start us, length us, event | category | flops | bytes accessed | tf_op | source)
XLA Modules:
  0.0 404.8 jit_solution(15349282896546801248)
XLA Ops:
  8.6 20.4 %all-gather.4.cloned.1.call-done = bf16[2048,256]{1,0:T(8,128)(2,1)} async-done(((bf16[512,256]{1,0:T(8,128)(2,1)}), bf16[2048,256]{1,0:T(8,128)(2,1)}) %all-gather.4.cloned.1.call-update) | async-done | bytes 1048592 | tf_op jit(solution)/shard_map/all_gather | solution.py:39
  29.1 6.0 %gather_fusion = bf16[1024,256]{1,0:T(8,128)(2,1)} fusion(bf16[2048,256]{1,0:T(8,128)(2,1)} %all-gather.4.cloned.1.call-done, s32[1024]{0:T(1024)S(1)} %broadcast_clamp_fusion), kind=kCustom, calls=%fused_computation | custom fusion | bytes 1052672 | tf_op jit(solution)/shard_map/gather | solution.py:41
  35.1 5.5 %all-to-all-start = ((bf16[8,128,256]{2,1,0:T(8,128)(2,1)}), bf16[8,128,256]{2,1,0:T(8,128)(2,1)S(1)}, u32[]{:S(2)}, u32[]{:S(2)}) async-start(bf16[8,128,256]{2,1,0:T(8,128)(2,1)} %bitcast.3), calls=%async_computation | async-start | bytes 1048576 | tf_op jit(solution)/shard_map/all_to_all | solution.py:44
  41.3 36.8 %all-gather = bf16[256,256]{1,0:T(8,128)(2,1)S(1)} all-gather(bf16[32,256]{1,0:T(8,128)(2,1)S(1)} %gather_fusion.1), channel_id=2, replica_groups=mesh['dom'=8,'tile'=4] {'dom'}, dimensions={0}, use_global_device_ids=true | all-gather | bytes 147456 | tf_op jit(solution)/shard_map/all_gather | solution.py:47
  78.3 5.6 %gather_fusion.2 = bf16[72,128,256]{2,1,0:T(8,128)(2,1)} fusion(bf16[26,128,256]{2,1,0:T(8,128)(2,1)S(1)} %bitcast.45, s32[1024]{0:T(1024)S(1)} %pad_clamp_fusion.1), kind=kCustom, calls=%fused_computation.2 | custom fusion | bytes 9437472 | tf_op jit(solution)/shard_map/gather | solution.py:53
  83.9 8.2 %convolution_bitcast_fusion.1 = f32[72,128,256]{1,2,0:T(8,128)} fusion(bf16[72,128,256]{2,1,0:T(8,128)(2,1)} %gather_fusion.2, bf16[72,128,128]{2,1,0:T(8,128)(2,1)} %param.13), kind=kOutput, calls=%fused_computation.8 | convolution fusion | flops 603979776 | bytes 16515072 | tf_op jit(solution)/shard_map/tij,tjf->tif/dot_general | solution.py:54
  92.1 9.7 %copy.33 = f32[72,128,256]{2,0,1:T(8,128)} copy(f32[72,128,256]{1,2,0:T(8,128)} %convolution_bitcast_fusion.1) | data formatting | bytes 18874368 | tf_op jit(solution)/shard_map/tij,tjf->tif/dot_general | solution.py:54
  101.8 6.9 %convolution_convert_fusion.1 = bf16[16,128,256]{2,0,1:T(8,128)(2,1)S(1)} fusion(f32[72,128,256]{2,0,1:T(8,128)} %copy.33, s32[72]{0:T(128)S(1)} %copy-done.8), kind=kOutput, calls=%fused_computation.11 | convolution fusion | flops 453510272 | bytes 10486048 | tf_op jit(solution)/shard_map/dt,tif->dif/dot_general | solution.py:56
  108.8 1.3 copy.34
  112.3 5.9 %all-reduce = bf16[2048]{0:T(1024)(128)(2,1)S(1)} all-reduce(bf16[2048]{0:T(1024)(128)(2,1)S(1)} %fusion.3), channel_id=4, replica_groups=mesh['dom'=8,'tile'=4] {'tile'}, use_global_device_ids=true, to_apply=%region_2.0.clone | all-reduce | flops 2048 | bytes 8192
  118.5 13.0 %reduce-scatter.4.cloned.1.call-done = bf16[512,256]{1,0:T(8,128)(2,1)} async-done(((bf16[2048,256]{1,0:T(8,128)(2,1)}), bf16[512,256]{1,0:T(8,128)(2,1)}) %reduce-scatter.4.cloned.1.call-update) | async-done | bytes 262160 | tf_op jit(solution)/shard_map/reduce_scatter | solution.py:64
  131.5 2.2 multiply_convert_fusion
  133.7 1.0 fusion.2
  135.7 2.0 fusion.14
  138.0 13.6 %all-gather.6.cloned.1.call-done = bf16[2048,256]{1,0:T(8,128)(2,1)} async-done(((bf16[512,256]{1,0:T(8,128)(2,1)}), bf16[2048,256]{1,0:T(8,128)(2,1)}) %all-gather.6.cloned.1.call-update) | async-done | bytes 1048592 | tf_op jit(solution)/shard_map/all_gather | solution.py:89
  151.6 6.8 %gather_fusion.3 = bf16[72,128,256]{2,1,0:T(8,128)(2,1)} fusion(bf16[16,128,256]{2,1,0:T(8,128)(2,1)} %bitcast.46, s32[1024]{0:T(1024)S(1)} %pad_clamp_fusion), kind=kCustom, calls=%fused_computation.3 | custom fusion | bytes 9437472 | tf_op jit(solution)/shard_map/gather | solution.py:90
  158.4 7.5 %convolution_bitcast_fusion = f32[72,128,256]{1,2,0:T(8,128)} fusion(bf16[72,128,256]{2,1,0:T(8,128)(2,1)} %gather_fusion.3, bf16[72,128,128]{2,1,0:T(8,128)(2,1)S(1)} %copy-done.3), kind=kOutput, calls=%fused_computation.7 | convolution fusion | flops 603979776 | bytes 16515072 | tf_op jit(solution)/shard_map/tij,tif->tjf/dot_general | solution.py:91
  165.9 9.7 %copy.36 = f32[72,128,256]{2,0,1:T(8,128)} copy(f32[72,128,256]{1,2,0:T(8,128)} %convolution_bitcast_fusion) | data formatting | bytes 18874368 | tf_op jit(solution)/shard_map/tij,tif->tjf/dot_general | solution.py:91
  175.6 7.8 %convolution_convert_fusion = bf16[26,128,256]{2,0,1:T(8,128)(2,1)S(1)} fusion(f32[72,128,256]{2,0,1:T(8,128)} %copy.36, s32[72]{0:T(128)S(1)} %copy-done.10), kind=kOutput, calls=%fused_computation.9 | convolution fusion | flops 736954176 | bytes 11141408 | tf_op jit(solution)/shard_map/st,tjf->sjf/dot_general | solution.py:93
  183.6 1.0 copy.38
  184.7 3.2 all-reduce.11.cloned.1.call-done
  187.9 36.2 %all-reduce.7.cloned.1.call-done = bf16[1280,256]{1,0:T(8,128)(2,1)} async-done(((bf16[1280,256]{1,0:T(8,128)(2,1)}), bf16[1280,256]{1,0:T(8,128)(2,1)}) %all-reduce.7.cloned.1.call-update) | async-done | bytes 655376 | tf_op jit(solution)/shard_map/psum | solution.py:99
  224.2 1.6 slice_convert_fusion
  226.0 1.3 copy.37
  228.2 5.6 %all-to-all-start.1 = ((bf16[8,128,256]{2,1,0:T(8,128)(2,1)}), bf16[8,128,256]{2,1,0:T(8,128)(2,1)S(1)}, u32[]{:S(2)}, u32[]{:S(2)}) async-start(bf16[8,128,256]{2,1,0:T(8,128)(2,1)} %bitcast.14), calls=%async_computation.3 | async-start | bytes 1048576 | tf_op jit(solution)/shard_map/all_to_all | solution.py:103
  233.9 71.3 %all-reduce.9.cloned.1.call-done = (f32[256,256]{0,1:T(8,128)}, f32[256,256]{0,1:T(8,128)}) async-done(((f32[256,256]{0,1:T(8,128)}, f32[256,256]{0,1:T(8,128)}), (f32[256,256]{0,1:T(8,128)}, f32[256,256]{0,1:T(8,128)})) %all-reduce.9.cloned.1.call-update) | async-done | bytes 524304 | tf_op jit(solution)/shard_map/psum | solution.py:10
  305.2 1.1 broadcast_multiply_fusion
  307.9 6.6 %scatter_custom_fusion = f32[2048,256]{1,0:T(8,128)S(1)} fusion(s32[1024]{0:T(1024)S(1)} %bitcast.53, bf16[1024,256]{1,0:T(8,128)(2,1)S(1)} %bitcast.50, f32[]{:T(128)} %constant.12.clone.1), kind=kCustom, calls=%fused_computation.21 | custom fusion | flops 524288 | bytes 2621444 | tf_op jit(solution)/shard_map/scatter-add | solution.py:110
  314.5 55.0 %reduce-scatter.8.cloned.1.call-done = f32[32,256]{1,0:T(8,128)} async-done(((f32[256,256]{1,0:T(8,128)}), f32[32,256]{1,0:T(8,128)}) %reduce-scatter.8.cloned.1.call-update) | async-done | bytes 32784 | tf_op jit(solution)/shard_map/reduce_scatter | solution.py:109
  369.5 1.8 scatter_fusion
  371.3 24.7 %reduce-scatter.6.cloned.1.call-done = bf16[512,256]{1,0:T(8,128)(2,1)} async-done(((bf16[2048,256]{1,0:T(8,128)(2,1)}), bf16[512,256]{1,0:T(8,128)(2,1)}) %reduce-scatter.6.cloned.1.call-update) | async-done | bytes 262160 | tf_op jit(solution)/shard_map/reduce_scatter | solution.py:96
  396.0 1.9 fusion.1
  (65 shorter events, 8.2 us)
Async XLA Ops:
  7.2 124.3 %copy-start = (bf16[256,256]{1,0:T(8,128)(2,1)S(1)}, bf16[256,256]{1,0:T(8,128)(2,1)}, u32[]{:S(2)}) copy-start(bf16[256,256]{1,0:T(8,128)(2,1)} %param.12) | copy-start | bytes 393220
  7.2 33.5 %copy-start.11 = (s32[32]{0:T(128)S(1)}, s32[32]{0:T(128)}, u32[]{:S(2)}) copy-start(s32[32]{0:T(128)} %param.17) | copy-start | bytes 388
  7.2 33.5 %copy-start.9 = (s32[72]{0:T(128)S(1)}, s32[72]{0:T(128)}, u32[]{:S(2)}) copy-start(s32[72]{0:T(128)} %param.15) | copy-start | bytes 868
  7.2 21.8 %all-gather.4.cloned.1.call-start = ((), (), s32[]{:S(2)}) async-start(), calls=%async_computation.5 | async-start | bytes 1310720 | tf_op jit(solution)/shard_map/all_gather | solution.py:39
  29.1 11.7 %copy-start.2 = (bf16[2048,256]{1,0:T(8,128)(2,1)S(1)}, bf16[2048,256]{1,0:T(8,128)(2,1)}, u32[]{:S(2)}) copy-start(bf16[2048,256]{1,0:T(8,128)(2,1)} %all-gather.4.cloned.1.call-done) | copy-start | bytes 3145732
  35.1 43.1 %all-to-all-start = ((bf16[8,128,256]{2,1,0:T(8,128)(2,1)}), bf16[8,128,256]{2,1,0:T(8,128)(2,1)S(1)}, u32[]{:S(2)}, u32[]{:S(2)}) async-start(bf16[8,128,256]{2,1,0:T(8,128)(2,1)} %bitcast.3), calls=%async_computation | async-start | bytes 1048576 | tf_op jit(solution)/shard_map/all_to_all | solution.py:44
  40.6 90.9 %reduce-scatter.4.cloned.1.call-start = ((), (), s32[]{:S(2)}) async-start(), calls=%async_computation.6 | async-start | bytes 1310720 | tf_op jit(solution)/shard_map/reduce_scatter | solution.py:64
  92.1 9.7 %copy-start.8 = (s32[72]{0:T(128)S(1)}, s32[72]{0:T(128)}, u32[]{:S(2)}) copy-start(s32[72]{0:T(128)} %param.14) | copy-start | bytes 868
  101.8 8.4 %copy-start.12 = (u32[32]{0:T(128)S(1)}, u32[32]{0:T(128)}, u32[]{:S(2)}) copy-start(u32[32]{0:T(128)} %constant.8) | copy-start | bytes 388
  108.7 2.7 copy-start.3
  108.8 9.6 %copy-start.4 = (bf16[512,256]{1,0:T(8,128)(2,1)S(1)}, bf16[512,256]{1,0:T(8,128)(2,1)}, u32[]{:S(2)}) copy-start(bf16[512,256]{1,0:T(8,128)(2,1)} %param.9) | copy-start | bytes 786436
  108.8 9.5 %copy-start.6 = (bf16[256,256]{1,0:T(8,128)(2,1)S(1)}, bf16[256,256]{1,0:T(8,128)(2,1)}, u32[]{:S(2)}) copy-start(bf16[256,256]{1,0:T(8,128)(2,1)} %param.11) | copy-start | bytes 393220
  110.2 41.4 %all-gather.6.cloned.1.call-start = ((), (), s32[]{:S(2)}) async-start(), calls=%async_computation.7 | async-start | bytes 1310720 | tf_op jit(solution)/shard_map/all_gather | solution.py:89
  134.7 53.1 %all-reduce.11.cloned.1.call-start = ((), (), s32[]{:S(2)}) async-start(), calls=%async_computation.12 | async-start | bytes 1048576 | tf_op jit(solution)/shard_map/psum | solution.py:10
  137.8 86.4 %all-reduce.7.cloned.1.call-start = ((), (), s32[]{:S(2)}) async-start(), calls=%async_computation.9 | async-start | bytes 1310720 | tf_op jit(solution)/shard_map/psum | solution.py:99
  165.9 9.8 %copy-start.10 = (s32[72]{0:T(128)S(1)}, s32[72]{0:T(128)}, u32[]{:S(2)}) copy-start(s32[72]{0:T(128)} %param.15) | copy-start | bytes 868
  184.6 120.5 %all-reduce.9.cloned.1.call-start = ((), (), s32[]{:S(2)}) async-start(), calls=%async_computation.11 | async-start | bytes 1048576 | tf_op jit(solution)/shard_map/psum | solution.py:10
  187.9 181.7 %reduce-scatter.8.cloned.1.call-start = ((), (), s32[]{:S(2)}) async-start(), calls=%async_computation.10 | async-start | bytes 294912 | tf_op jit(solution)/shard_map/reduce_scatter | solution.py:109
  225.8 170.2 %reduce-scatter.6.cloned.1.call-start = ((), (), s32[]{:S(2)}) async-start(), calls=%async_computation.8 | async-start | bytes 1310720 | tf_op jit(solution)/shard_map/reduce_scatter | solution.py:96
  226.0 1.4 copy-start.5
  228.2 167.8 %copy-start.7 = (bf16[256,256]{1,0:T(8,128)(2,1)S(1)}, bf16[256,256]{1,0:T(8,128)(2,1)}, u32[]{:S(2)}) copy-start(bf16[256,256]{1,0:T(8,128)(2,1)} %param.11) | copy-start | bytes 393220
  228.2 79.7 %all-to-all-start.1 = ((bf16[8,128,256]{2,1,0:T(8,128)(2,1)}), bf16[8,128,256]{2,1,0:T(8,128)(2,1)S(1)}, u32[]{:S(2)}, u32[]{:S(2)}) async-start(bf16[8,128,256]{2,1,0:T(8,128)(2,1)} %bitcast.14), calls=%async_computation.3 | async-start | bytes 1048576 | tf_op jit(solution)/shard_map/all_to_all | solution.py:103
  233.8 164.1 %copy-start.1 = (bf16[256,256]{1,0:T(8,128)(2,1)S(1)}, bf16[256,256]{1,0:T(8,128)(2,1)}, u32[]{:S(2)}) copy-start(bf16[256,256]{1,0:T(8,128)(2,1)} %param.12) | copy-start | bytes 393220
Sparse Core Ops, SparseCore 0:
  9.6 19.4 all-gather.3
  110.3 21.1 reduce-scatter.3
  134.8 16.7 all-gather.5
  154.6 33.2 all-reduce.10
  190.2 33.9 all-reduce.6
  227.9 77.2 all-reduce.8
  309.1 60.4 reduce-scatter.7
  372.1 23.9 reduce-scatter.5
